TPU v7x, 32 devices: a whole 2x2x4 slice. The times are simulated.
32 devices in a mesh: px: 8 (over y, x, core), py: 4 (over z).
Axes of the slice: x: 2, y: 2, z: 4, core: 2. Of those that a mesh axis runs over, the one named last changes fastest.
Arguments:
- node_features: bfloat16 [16384, 192], P(('px', 'py')), may hold values from -6 to 6
- edge_source: int32 [32, 3072], P(('px', 'py')), may hold values from 0 to 767
- edge_target: int32 [32, 3072], P(('px', 'py')), may hold values from 0 to 512, as said below
- halo_send: int32 [32, 64], P(('px', 'py')), may hold values from 0 to 511
- edge_weight_in: bfloat16 [384, 192], replicated, may hold values from -0.3125 to 0.3125
- edge_bias: float32 [192], replicated, may hold values from -4 to 4
- edge_weight_out: bfloat16 [192, 192], replicated, may hold values from -0.4375 to 0.4375
- node_weight_in: bfloat16 [384, 192], replicated, may hold values from -0.3125 to 0.3125
- node_bias: float32 [192], replicated, may hold values from -4 to 4
- node_weight_out: bfloat16 [192, 192], replicated, may hold values from -0.4375 to 0.4375
- cluster_owner: int32 [16384, 1], P(('px', 'py')), may hold values from 0 to 3; in each aligned block of 512 rows (0 to 511, 512 to 1023, ...) at most 256 rows name the same one
- cluster_member: int32 [16384], P(('px', 'py')), may hold values from 0 to 63
- coarse_send: int32 [32, 16], P(('px', 'py')), may hold values from 0 to 63
- coarse_source: int32 [32, 384], P(('px', 'py')), may hold values from 0 to 127
- coarse_target: int32 [32, 384], P(('px', 'py')), may hold values from 0 to 64, as said below
- coarse_edge_in: bfloat16 [384, 192], replicated, may hold values from -0.3125 to 0.3125
- coarse_edge_bias: float32 [192], replicated, may hold values from -4 to 4
- coarse_edge_out: bfloat16 [192, 192], replicated, may hold values from -0.4375 to 0.4375
- coarse_node_in: bfloat16 [384, 192], replicated, may hold values from -0.3125 to 0.3125
- coarse_node_bias: float32 [192], replicated, may hold values from -4 to 4
- coarse_node_out: bfloat16 [192, 192], replicated, may hold values from -0.4375 to 0.4375
Outputs:
- node_updated: bfloat16 [16384, 192], P(('px', 'py'))
- cluster_updated: bfloat16 [2048, 192], P(('px', 'py'))
Inputs may be any that keep to these rules, and one draw needn't show every extreme that they name: `edge_target`: each device's slots hold a target node of that device; padding slots hold 512 and stand only at the end of a device's list; at least three quarters of each device's slots are live and some device has no padding. `coarse_target`: each device's slots hold a target cluster of that device; padding slots hold 64 and stand only at the end of a device's list; at least three quarters of each device's slots are live and some device has no padding. `cluster_owner`: at most 256 nodes of one device have the same owner, and in every draw some device has exactly 256 nodes with one owner.
All inputs are finite; a program needn't handle non-finite values.
Results may differ from a plain program's by a relative error of at most 0.014.
Values may be sent and summed in bfloat16 or wider, within the bound.
A program may use at most 64 MiB of HBM per device.

v0:
```python
import math

import jax
import jax.numpy as jnp
from jax import lax
from jax.sharding import PartitionSpec as P

CLUST_DEV = 64


def padded_2(block, sides, width):
    for axis, dim in sides:
        count = lax.axis_size(axis)
        forward = [(i, i + 1) for i in range(count - 1)]
        backward = [(target, source) for source, target in forward]
        low = lax.ppermute(
            lax.slice_in_dim(block, block.shape[dim] - width, None, axis=dim), axis, forward
        )
        high = lax.ppermute(lax.slice_in_dim(block, 0, width, axis=dim), axis, backward)
        block = jnp.concatenate([low, block, high], axis=dim)
    return block


def normed(values):
    center = values - jnp.mean(values, axis=-1, keepdims=True)
    return center * lax.rsqrt(jnp.mean(center * center, axis=-1, keepdims=True) + 1e-05)


def rim_rows(padded):
    return (padded[0, 1], padded[2, 1], padded[1, 0], padded[1, 2])


def pick_rows(row_ids, table):
    selector = (row_ids[:, None] == lax.broadcasted_iota(jnp.int32, (1, table.shape[0]), 1)).astype(
        jnp.bfloat16
    )
    return jnp.dot(selector, table, preferred_element_type=jnp.float32).astype(jnp.bfloat16)


def one_round(features, lookup_table, sources, targets, weights):
    weight_in, bias, weight_out, node_in, node_bias, node_out = weights
    amount = features.shape[0]
    edge_total = sources.shape[0]
    block_rows = math.gcd(edge_total, 768)
    groups = edge_total // block_rows

    def add_block(totals, pieces):
        block_sources, block_targets = pieces
        paired = jnp.concatenate(
            [pick_rows(block_sources, lookup_table), pick_rows(block_targets, features)], axis=1
        )
        hidden = jax.nn.silu(
            jnp.dot(paired, weight_in, preferred_element_type=jnp.float32) + bias
        ).astype(jnp.bfloat16)
        message = normed(jnp.dot(hidden, weight_out, preferred_element_type=jnp.float32))
        upper = message.astype(jnp.bfloat16)
        lower = (message - upper.astype(jnp.float32)).astype(jnp.bfloat16)
        spread = (lax.broadcasted_iota(jnp.int32, (amount, 1), 0) == block_targets[None, :]).astype(
            jnp.bfloat16
        )
        added = jnp.dot(spread, upper, preferred_element_type=jnp.float32) + jnp.dot(
            spread, lower, preferred_element_type=jnp.float32
        )
        return (totals + added, None)

    totals, unused = lax.scan(
        add_block,
        jnp.zeros((amount, features.shape[1]), jnp.float32),
        (sources.reshape(groups, block_rows), targets.reshape(groups, block_rows)),
    )
    joined = jnp.concatenate([features, totals.astype(jnp.bfloat16)], axis=1)
    node_hidden = jax.nn.silu(
        jnp.dot(joined, node_in, preferred_element_type=jnp.float32) + node_bias
    ).astype(jnp.bfloat16)
    return (
        features.astype(jnp.float32)
        + normed(jnp.dot(node_hidden, node_out, preferred_element_type=jnp.float32))
    ).astype(jnp.bfloat16)


def body(
    node_features,
    edge_source,
    edge_target,
    halo_send,
    edge_weight_in,
    edge_bias,
    edge_weight_out,
    node_weight_in,
    node_bias,
    node_weight_out,
    cluster_owner,
    cluster_member,
    coarse_send,
    coarse_source,
    coarse_target,
    coarse_edge_in,
    coarse_edge_bias,
    coarse_edge_out,
    coarse_node_in,
    coarse_node_bias,
    coarse_node_out,
):
    shared_nodes = pick_rows(halo_send[0], node_features)
    padded = padded_2(shared_nodes[None, None], (("px", 0), ("py", 1)), 1)
    lookup_table = jnp.concatenate((node_features,) + rim_rows(padded), axis=0)
    node_updated = one_round(
        node_features,
        lookup_table,
        edge_source[0],
        edge_target[0],
        (edge_weight_in, edge_bias, edge_weight_out, node_weight_in, node_bias, node_weight_out),
    )
    owners = cluster_owner[:, 0]
    owner_count = lax.axis_size("py")
    node_count = node_updated.shape[0]
    capacity = 2 * node_count // owner_count
    onehot = (owners[:, None] == lax.broadcasted_iota(jnp.int32, (1, owner_count), 1)).astype(
        jnp.float32
    )
    lower_ones = (
        lax.broadcasted_iota(jnp.int32, (node_count, node_count), 0)
        >= lax.broadcasted_iota(jnp.int32, (node_count, node_count), 1)
    ).astype(jnp.float32)
    running = jnp.dot(
        lower_ones, onehot, precision=lax.Precision.HIGHEST, preferred_element_type=jnp.float32
    )
    ranking = (jnp.sum(running * onehot, axis=1) - 1.0).astype(jnp.int32)
    position = owners * capacity + ranking
    placing = lax.broadcasted_iota(jnp.int32, (owner_count * capacity, 1), 0) == position[None, :]
    buffer = jnp.dot(
        placing.astype(jnp.bfloat16), node_updated, preferred_element_type=jnp.float32
    ).astype(jnp.bfloat16)
    shifted_ids = jnp.dot(
        placing.astype(jnp.float32),
        (cluster_member + 1).astype(jnp.float32)[:, None],
        precision=lax.Precision.HIGHEST,
        preferred_element_type=jnp.float32,
    )
    member_ids = shifted_ids[:, 0].astype(jnp.int32) - 1
    arrived, arrived_ids = (
        lax.all_to_all(buffer, "py", split_axis=0, concat_axis=0, tiled=True),
        lax.all_to_all(member_ids, "py", split_axis=0, concat_axis=0, tiled=True),
    )
    select = arrived_ids[None, :] == lax.broadcasted_iota(jnp.int32, (CLUST_DEV, 1), 0)
    pooled = jnp.dot(select.astype(jnp.bfloat16), arrived, preferred_element_type=jnp.float32)
    counts = jnp.sum(select.astype(jnp.float32), axis=1)
    coarse = (pooled / jnp.maximum(counts, 1.0)[:, None]).astype(jnp.bfloat16)
    coarse_shared = pick_rows(coarse_send[0], coarse)
    coarse_padded = padded_2(coarse_shared[None, None], (("px", 0), ("py", 1)), 1)
    coarse_table = jnp.concatenate((coarse,) + rim_rows(coarse_padded), axis=0)
    cluster_updated = one_round(
        coarse,
        coarse_table,
        coarse_source[0],
        coarse_target[0],
        (
            coarse_edge_in,
            coarse_edge_bias,
            coarse_edge_out,
            coarse_node_in,
            coarse_node_bias,
            coarse_node_out,
        ),
    )
    return (node_updated, cluster_updated)


def solution(mesh):
    placed = (
        P(("px", "py"), None),
        P(("px", "py"), None),
        P(("px", "py"), None),
        P(("px", "py"), None),
        P(),
        P(),
        P(),
        P(),
        P(),
        P(),
        P(("px", "py"), None),
        P(("px", "py")),
        P(("px", "py"), None),
        P(("px", "py"), None),
        P(("px", "py"), None),
        P(),
        P(),
        P(),
        P(),
        P(),
        P(),
    )
    return jax.shard_map(
        body,
        mesh=mesh,
        in_specs=placed,
        out_specs=(P(("px", "py"), None), P(("px", "py"), None)),
        check_vma=False,
    )
```

profile of v0, /device:TPU:3, one launch (start us, length us, event | category | flops | bytes accessed | tf_op | source)
XLA Modules:
  0.0 78.7 jit_solution(12001590389462845622)
XLA Ops:
  0.7 1.2 %fusion.34 = bf16[1,1,64,192]{3,2,1,0:T(8,128)(2,1)S(1)} fusion(bf16[512,192]{0,1:T(8,128)(2,1)} %param.23, s32[64]{0:T(128)} %bitcast.75), kind=kOutput, calls=%fused_computation.50 | convolution fusion | flops 12627968 | bytes 221440 | tf_op jit(solution)/shard_map/dot_general | solution.py:37
  1.9 3.7 %collective-permute-start = (bf16[1,1,64,192]{3,2,1,0:T(8,128)(2,1)S(1)}, bf16[1,1,64,192]{3,2,1,0:T(8,128)(2,1)S(1)}, u32[]{:S(2)}, u32[]{:S(2)}) collective-permute-start(bf16[1,1,64,192]{3,2,1,0:T(8,128)(2,1)S(1)} %fusion.34), channel_id=1, source_target_pairs={{0,4},{4,8},{8,12},{12,16},{16,20},{20,24},{24,28},{1,5},{5,9},{9,... | collective-permute-start | bytes 73736 | tf_op jit(solution)/shard_map/ppermute | solution.py:16
  5.5 1.9 %collective-permute-start.1 = (bf16[1,1,64,192]{3,2,1,0:T(8,128)(2,1)S(1)}, bf16[1,1,64,192]{3,2,1,0:T(8,128)(2,1)S(1)}, u32[]{:S(2)}, u32[]{:S(2)}) collective-permute-start(bf16[1,1,64,192]{3,2,1,0:T(8,128)(2,1)S(1)} %fusion.34), channel_id=1, source_target_pairs={{4,0},{8,4},{12,8},{16,12},{20,16},{24,20},{28,24},{5,1},{9,5},{13... | collective-permute-start | bytes 73736 | tf_op jit(solution)/shard_map/ppermute | solution.py:19
  7.5 1.0 %fusion.36 = f32[512]{0:T(512)S(1)} fusion(s32[512]{0:T(512)} %bitcast.72), kind=kOutput, calls=%fused_computation.54 | convolution fusion | flops 2366976 | bytes 4096 | tf_op jit(solution)/shard_map/dot_general | solution.py:125
  8.5 0.7 convert_add_fusion.1
  9.2 0.7 add_convert_fusion.2
  9.9 1.0 %fusion.30 = f32[1,1024]{1,0:T(1,128)S(1)} fusion(f32[512,1]{0,1:T(1,128)S(1)} %bitcast.74, s32[512]{0:T(512)S(1)} %convert_add_fusion.1), kind=kOutput, calls=%fused_computation.38 | convolution fusion | flops 6815744 | bytes 8192 | tf_op jit(solution)/shard_map/dot_general | solution.py:134
  10.9 0.6 convert_add_fusion
  11.5 4.6 %all-to-all-start = ((s32[4,256,1]{1,2,0:T(1,128)}), s32[4,256,1]{1,2,0:T(1,128)S(1)}, u32[]{:S(2)}, u32[]{:S(2)}) async-start(s32[4,256,1]{1,2,0:T(1,128)} %bitcast.9), calls=%async_computation | async-start | bytes 8192 | tf_op jit(solution)/shard_map/all_to_all | solution.py:143
  16.1 0.1 copy.32
  16.3 0.6 broadcast.169
  16.9 0.7 reduce.12
  17.7 0.7 reduce.13
  18.4 3.4 %collective-permute-start.2 = (bf16[3,1,64,192]{3,2,1,0:T(8,128)(2,1)S(1)}, bf16[3,1,64,192]{3,2,1,0:T(8,128)(2,1)S(1)}, u32[]{:S(2)}, u32[]{:S(2)}) collective-permute-start(bf16[3,1,64,192]{3,2,1,0:T(8,128)(2,1)S(1)} %pad_maximum_fusion), channel_id=1, source_target_pairs={{0,1},{1,2},{2,3},{4,5},{5,6},{6,7},{8,9},{9,10},{10,11},{12,13},{... | collective-permute-start | bytes 221192 | tf_op jit(solution)/shard_map/ppermute | solution.py:16
  21.8 1.3 %collective-permute-start.3 = (bf16[3,1,64,192]{3,2,1,0:T(8,128)(2,1)S(1)}, bf16[3,1,64,192]{3,2,1,0:T(8,128)(2,1)S(1)}, u32[]{:S(2)}, u32[]{:S(2)}) collective-permute-start(bf16[3,1,64,192]{3,2,1,0:T(8,128)(2,1)S(1)} %pad_maximum_fusion), channel_id=1, source_target_pairs={{1,0},{2,1},{3,2},{5,4},{6,5},{7,6},{9,8},{10,9},{11,10},{13,12},{... | collective-permute-start | bytes 221192 | tf_op jit(solution)/shard_map/ppermute | solution.py:19
  23.2 0.3 collective-permute-done.2
  23.4 3.7 %collective-permute-done.3 = bf16[3,1,64,192]{3,2,1,0:T(8,128)(2,1)S(1)} collective-permute-done((bf16[3,1,64,192]{3,2,1,0:T(8,128)(2,1)S(1)}, bf16[3,1,64,192]{3,2,1,0:T(8,128)(2,1)S(1)}, u32[]{:S(2)}, u32[]{:S(2)}) %collective-permute-start.3) | collective-permute-done | bytes 73760 | tf_op jit(solution)/shard_map/ppermute | solution.py:19
  27.2 12.6 %while.3 = (s32[]{:T(128)}, f32[512,192]{0,1:T(8,128)S(1)}, s32[4,768]{1,0:T(4,128)S(1)}, s32[4,768]{1,0:T(4,128)S(1)}, bf16[768,192]{1,0:T(8,128)(2,1)S(1)}, /*...) while((s32[]{:T(128)}, f32[512,192]{0,1:T(8,128)S(1)}, ...), condition=%wide.region_3.4_spmd.clone, body=%wide.region_0.3_spmd.clone.sunk | while | flops 855687936 | bytes 5883771 | solution.py:66
  27.3 0.6 fusion.136
  27.8 0.7 fusion.137
  28.6 0.6 fusion.138
  29.3 0.5 fusion.139
  29.8 0.6 fusion.140
  30.4 0.6 fusion.136
  31.0 0.7 fusion.137
  31.7 0.6 fusion.138
  32.4 0.5 fusion.139
  32.9 0.6 fusion.140
  33.5 0.6 fusion.136
  34.1 0.7 fusion.137
  34.8 0.6 fusion.138
  35.5 0.5 fusion.139
  36.0 0.6 fusion.140
  36.7 0.6 fusion.136
  37.3 0.7 fusion.137
  38.0 0.6 fusion.138
  38.7 0.5 fusion.139
  39.2 0.6 fusion.140
  39.8 0.8 %copy-done.11 = bf16[192,192]{1,0:T(8,128)(2,1)S(1)} copy-done((bf16[192,192]{1,0:T(8,128)(2,1)S(1)}, bf16[192,192]{1,0:T(8,128)(2,1)}, u32[]{:S(2)}) %copy-start.11) | copy-done | bytes 73752
  40.7 0.5 fusion.95
  41.4 0.6 fusion.31
  42.0 0.1 copy-done.2
  42.1 0.8 copy.39
  42.8 3.6 %all-to-all-start.1 = ((bf16[4,256,192]{1,2,0:T(8,128)(2,1)}), bf16[4,256,192]{1,2,0:T(8,128)(2,1)S(1)}, u32[]{:S(2)}, u32[]{:S(2)}) async-start(bf16[4,256,192]{1,2,0:T(8,128)(2,1)} %bitcast.57), calls=%async_computation.1 | async-start | bytes 786432 | tf_op jit(solution)/shard_map/all_to_all | solution.py:142
  46.5 0.1 convert_reduce_fusion
  46.6 8.8 %all-to-all-done.1 = bf16[4,256,192]{1,2,0:T(8,128)(2,1)S(1)} async-done(((bf16[4,256,192]{1,2,0:T(8,128)(2,1)}), bf16[4,256,192]{1,2,0:T(8,128)(2,1)S(1)}, u32[]{:S(2)}, u32[]{:S(2)}) %all-to-all-start.1) | async-done | bytes 393248 | tf_op jit(solution)/shard_map/all_to_all | solution.py:142
  55.5 0.3 constant_dynamic-update-slice_fusion.5
  55.8 0.3 copy-done.18
  56.1 0.2 fusion.35
  56.3 6.6 %collective-permute-start.4 = (bf16[1,1,16,192]{3,2,1,0:T(8,128)(2,1)S(1)}, bf16[1,1,16,192]{3,2,1,0:T(8,128)(2,1)S(1)}, u32[]{:S(2)}, u32[]{:S(2)}) collective-permute-start(bf16[1,1,16,192]{3,2,1,0:T(8,128)(2,1)S(1)} %fusion.35), channel_id=1, source_target_pairs={{0,4},{4,8},{8,12},{12,16},{16,20},{20,24},{24,28},{1,5},{5,9},{9,... | collective-permute-start | bytes 18440 | tf_op jit(solution)/shard_map/ppermute | solution.py:16
  62.9 1.9 %collective-permute-start.5 = (bf16[1,1,16,192]{3,2,1,0:T(8,128)(2,1)S(1)}, bf16[1,1,16,192]{3,2,1,0:T(8,128)(2,1)S(1)}, u32[]{:S(2)}, u32[]{:S(2)}) collective-permute-start(bf16[1,1,16,192]{3,2,1,0:T(8,128)(2,1)S(1)} %fusion.35), channel_id=1, source_target_pairs={{4,0},{8,4},{12,8},{16,12},{20,16},{24,20},{28,24},{5,1},{9,5},{13... | collective-permute-start | bytes 18440 | tf_op jit(solution)/shard_map/ppermute | solution.py:19
  64.8 0.3 convolution_convert_fusion
  65.1 3.6 %collective-permute-done.5 = bf16[1,1,16,192]{3,2,1,0:T(8,128)(2,1)S(1)} collective-permute-done((bf16[1,1,16,192]{3,2,1,0:T(8,128)(2,1)S(1)}, bf16[1,1,16,192]{3,2,1,0:T(8,128)(2,1)S(1)}, u32[]{:S(2)}, u32[]{:S(2)}) %collective-permute-start.5) | collective-permute-done | bytes 6176 | tf_op jit(solution)/shard_map/ppermute | solution.py:19
  68.8 2.2 %collective-permute-start.6 = (bf16[3,1,16,192]{3,2,1,0:T(8,128)(2,1)S(1)}, bf16[3,1,16,192]{3,2,1,0:T(8,128)(2,1)S(1)}, u32[]{:S(2)}, u32[]{:S(2)}) collective-permute-start(bf16[3,1,16,192]{3,2,1,0:T(8,128)(2,1)S(1)} %pad_maximum_fusion.1), channel_id=1, source_target_pairs={{0,1},{1,2},{2,3},{4,5},{5,6},{6,7},{8,9},{9,10},{10,11},{12,13},{... | collective-permute-start | bytes 55304 | tf_op jit(solution)/shard_map/ppermute | solution.py:16
  70.9 1.3 %collective-permute-start.7 = (bf16[3,1,16,192]{3,2,1,0:T(8,128)(2,1)S(1)}, bf16[3,1,16,192]{3,2,1,0:T(8,128)(2,1)S(1)}, u32[]{:S(2)}, u32[]{:S(2)}) collective-permute-start(bf16[3,1,16,192]{3,2,1,0:T(8,128)(2,1)S(1)} %pad_maximum_fusion.1), channel_id=1, source_target_pairs={{1,0},{2,1},{3,2},{5,4},{6,5},{7,6},{9,8},{10,9},{11,10},{13,12},{... | collective-permute-start | bytes 55304 | tf_op jit(solution)/shard_map/ppermute | solution.py:19
  72.3 3.2 %collective-permute-done.7 = bf16[3,1,16,192]{3,2,1,0:T(8,128)(2,1)S(1)} collective-permute-done((bf16[3,1,16,192]{3,2,1,0:T(8,128)(2,1)S(1)}, bf16[3,1,16,192]{3,2,1,0:T(8,128)(2,1)S(1)}, u32[]{:S(2)}, u32[]{:S(2)}) %collective-permute-start.7) | collective-permute-done | bytes 18464 | tf_op jit(solution)/shard_map/ppermute | solution.py:19
  75.5 0.3 convolution_convert_fusion.1
  75.8 0.5 fusion.98
  76.4 0.2 fusion.57
  76.6 0.2 fusion.32
  76.8 0.4 copy-done.9
  77.3 0.4 fusion.101
  77.7 0.2 multiply_reduce_fusion.3
  77.9 0.7 add_convert_fusion.1
  (83 shorter events, 1.1 us)
Async XLA Ops:
  0.6 39.2 %copy-start = (bf16[384,192]{0,1:T(8,128)(2,1)S(1)}, bf16[384,192]{0,1:T(8,128)(2,1)}, u32[]{:S(2)}) copy-start(bf16[384,192]{0,1:T(8,128)(2,1)} %param.30) | copy-start | bytes 442372
  0.6 15.4 %copy-start.1 = (bf16[512,192]{0,1:T(8,128)(2,1)S(1)}, bf16[512,192]{0,1:T(8,128)(2,1)}, u32[]{:S(2)}) copy-start(bf16[512,192]{0,1:T(8,128)(2,1)} %param.23) | copy-start | bytes 589828
  1.9 16.5 %collective-permute-start = (bf16[1,1,64,192]{3,2,1,0:T(8,128)(2,1)S(1)}, bf16[1,1,64,192]{3,2,1,0:T(8,128)(2,1)S(1)}, u32[]{:S(2)}, u32[]{:S(2)}) collective-permute-start(bf16[1,1,64,192]{3,2,1,0:T(8,128)(2,1)S(1)} %fusion.34), channel_id=1, source_target_pairs={{0,4},{4,8},{8,12},{12,16},{16,20},{20,24},{24,28},{1,5},{5,9},{9,... | collective-permute-start | bytes 73736 | tf_op jit(solution)/shard_map/ppermute | solution.py:16
  5.5 12.9 %collective-permute-start.1 = (bf16[1,1,64,192]{3,2,1,0:T(8,128)(2,1)S(1)}, bf16[1,1,64,192]{3,2,1,0:T(8,128)(2,1)S(1)}, u32[]{:S(2)}, u32[]{:S(2)}) collective-permute-start(bf16[1,1,64,192]{3,2,1,0:T(8,128)(2,1)S(1)} %fusion.34), channel_id=1, source_target_pairs={{4,0},{8,4},{12,8},{16,12},{20,16},{24,20},{28,24},{5,1},{9,5},{13... | collective-permute-start | bytes 73736 | tf_op jit(solution)/shard_map/ppermute | solution.py:19
  10.9 6.0 %copy-start.3 = (s32[1,3072]{1,0:T(1,128)S(1)}, s32[1,3072]{1,0:T(1,128)}, u32[]{:S(2)}) copy-start(s32[1,3072]{1,0:T(1,128)} %param.25) | copy-start | bytes 36868
  10.9 6.8 %copy-start.4 = (s32[1,3072]{1,0:T(1,128)S(1)}, s32[1,3072]{1,0:T(1,128)}, u32[]{:S(2)}) copy-start(s32[1,3072]{1,0:T(1,128)} %param.24) | copy-start | bytes 36868
  11.5 31.3 %all-to-all-start = ((s32[4,256,1]{1,2,0:T(1,128)}), s32[4,256,1]{1,2,0:T(1,128)S(1)}, u32[]{:S(2)}, u32[]{:S(2)}) async-start(s32[4,256,1]{1,2,0:T(1,128)} %bitcast.9), calls=%async_computation | async-start | bytes 8192 | tf_op jit(solution)/shard_map/all_to_all | solution.py:143
  16.2 11.0 %copy-start.7 = (bf16[384,192]{0,1:T(8,128)(2,1)S(1)}, bf16[384,192]{0,1:T(8,128)(2,1)}, u32[]{:S(2)}) copy-start(bf16[384,192]{0,1:T(8,128)(2,1)} %param.27) | copy-start | bytes 442372
  16.2 11.0 %copy-start.10 = (bf16[192,192]{1,0:T(8,128)(2,1)S(1)}, bf16[192,192]{1,0:T(8,128)(2,1)}, u32[]{:S(2)}) copy-start(bf16[192,192]{1,0:T(8,128)(2,1)} %param.29) | copy-start | bytes 221188
  16.3 10.9 %copy-start.14 = (f32[192]{0:T(256)S(1)}, f32[192]{0:T(256)}, u32[]{:S(2)}) copy-start(f32[192]{0:T(256)} %param.28) | copy-start | bytes 2308
  18.4 5.0 %collective-permute-start.2 = (bf16[3,1,64,192]{3,2,1,0:T(8,128)(2,1)S(1)}, bf16[3,1,64,192]{3,2,1,0:T(8,128)(2,1)S(1)}, u32[]{:S(2)}, u32[]{:S(2)}) collective-permute-start(bf16[3,1,64,192]{3,2,1,0:T(8,128)(2,1)S(1)} %pad_maximum_fusion), channel_id=1, source_target_pairs={{0,1},{1,2},{2,3},{4,5},{5,6},{6,7},{8,9},{9,10},{10,11},{12,13},{... | collective-permute-start | bytes 221192 | tf_op jit(solution)/shard_map/ppermute | solution.py:16
  21.8 5.4 %collective-permute-start.3 = (bf16[3,1,64,192]{3,2,1,0:T(8,128)(2,1)S(1)}, bf16[3,1,64,192]{3,2,1,0:T(8,128)(2,1)S(1)}, u32[]{:S(2)}, u32[]{:S(2)}) collective-permute-start(bf16[3,1,64,192]{3,2,1,0:T(8,128)(2,1)S(1)} %pad_maximum_fusion), channel_id=1, source_target_pairs={{1,0},{2,1},{3,2},{5,4},{6,5},{7,6},{9,8},{10,9},{11,10},{13,12},{... | collective-permute-start | bytes 221192 | tf_op jit(solution)/shard_map/ppermute | solution.py:19
  39.8 0.9 %copy-start.11 = (bf16[192,192]{1,0:T(8,128)(2,1)S(1)}, bf16[192,192]{1,0:T(8,128)(2,1)}, u32[]{:S(2)}) copy-start(bf16[192,192]{1,0:T(8,128)(2,1)} %param.32) | copy-start | bytes 221188
  39.8 0.9 %copy-start.15 = (f32[192]{0:T(256)S(1)}, f32[192]{0:T(256)}, u32[]{:S(2)}) copy-start(f32[192]{0:T(256)} %param.31) | copy-start | bytes 2308
  41.4 0.7 copy-start.2
  42.8 3.6 %copy-start.5 = (s32[1,384]{1,0:T(1,128)S(1)}, s32[1,384]{1,0:T(1,128)}, u32[]{:S(2)}) copy-start(s32[1,384]{1,0:T(1,128)} %param.36) | copy-start | bytes 4612
  42.8 3.6 %copy-start.6 = (s32[1,384]{1,0:T(1,128)S(1)}, s32[1,384]{1,0:T(1,128)}, u32[]{:S(2)}) copy-start(s32[1,384]{1,0:T(1,128)} %param.37) | copy-start | bytes 4612
  42.8 12.6 %all-to-all-start.1 = ((bf16[4,256,192]{1,2,0:T(8,128)(2,1)}), bf16[4,256,192]{1,2,0:T(8,128)(2,1)S(1)}, u32[]{:S(2)}, u32[]{:S(2)}) async-start(bf16[4,256,192]{1,2,0:T(8,128)(2,1)} %bitcast.57), calls=%async_computation.1 | async-start | bytes 786432 | tf_op jit(solution)/shard_map/all_to_all | solution.py:142
  55.4 0.7 copy-start.18
  55.5 20.3 %copy-start.8 = (bf16[384,192]{0,1:T(8,128)(2,1)S(1)}, bf16[384,192]{0,1:T(8,128)(2,1)}, u32[]{:S(2)}) copy-start(bf16[384,192]{0,1:T(8,128)(2,1)} %param.38) | copy-start | bytes 442372
  55.5 20.3 %copy-start.12 = (bf16[192,192]{1,0:T(8,128)(2,1)S(1)}, bf16[192,192]{1,0:T(8,128)(2,1)}, u32[]{:S(2)}) copy-start(bf16[192,192]{1,0:T(8,128)(2,1)} %param.40) | copy-start | bytes 221188
  55.5 20.3 %copy-start.16 = (f32[192]{0:T(256)S(1)}, f32[192]{0:T(256)}, u32[]{:S(2)}) copy-start(f32[192]{0:T(256)} %param.39) | copy-start | bytes 2308
  56.3 8.8 %collective-permute-start.4 = (bf16[1,1,16,192]{3,2,1,0:T(8,128)(2,1)S(1)}, bf16[1,1,16,192]{3,2,1,0:T(8,128)(2,1)S(1)}, u32[]{:S(2)}, u32[]{:S(2)}) collective-permute-start(bf16[1,1,16,192]{3,2,1,0:T(8,128)(2,1)S(1)} %fusion.35), channel_id=1, source_target_pairs={{0,4},{4,8},{8,12},{12,16},{16,20},{20,24},{24,28},{1,5},{5,9},{9,... | collective-permute-start | bytes 18440 | tf_op jit(solution)/shard_map/ppermute | solution.py:16
  62.9 5.9 %collective-permute-start.5 = (bf16[1,1,16,192]{3,2,1,0:T(8,128)(2,1)S(1)}, bf16[1,1,16,192]{3,2,1,0:T(8,128)(2,1)S(1)}, u32[]{:S(2)}, u32[]{:S(2)}) collective-permute-start(bf16[1,1,16,192]{3,2,1,0:T(8,128)(2,1)S(1)} %fusion.35), channel_id=1, source_target_pairs={{4,0},{8,4},{12,8},{16,12},{20,16},{24,20},{28,24},{5,1},{9,5},{13... | collective-permute-start | bytes 18440 | tf_op jit(solution)/shard_map/ppermute | solution.py:19
  68.8 3.5 %collective-permute-start.6 = (bf16[3,1,16,192]{3,2,1,0:T(8,128)(2,1)S(1)}, bf16[3,1,16,192]{3,2,1,0:T(8,128)(2,1)S(1)}, u32[]{:S(2)}, u32[]{:S(2)}) collective-permute-start(bf16[3,1,16,192]{3,2,1,0:T(8,128)(2,1)S(1)} %pad_maximum_fusion.1), channel_id=1, source_target_pairs={{0,1},{1,2},{2,3},{4,5},{5,6},{6,7},{8,9},{9,10},{10,11},{12,13},{... | collective-permute-start | bytes 55304 | tf_op jit(solution)/shard_map/ppermute | solution.py:16
  70.9 4.6 %collective-permute-start.7 = (bf16[3,1,16,192]{3,2,1,0:T(8,128)(2,1)S(1)}, bf16[3,1,16,192]{3,2,1,0:T(8,128)(2,1)S(1)}, u32[]{:S(2)}, u32[]{:S(2)}) collective-permute-start(bf16[3,1,16,192]{3,2,1,0:T(8,128)(2,1)S(1)} %pad_maximum_fusion.1), channel_id=1, source_target_pairs={{1,0},{2,1},{3,2},{5,4},{6,5},{7,6},{9,8},{10,9},{11,10},{13,12},{... | collective-permute-start | bytes 55304 | tf_op jit(solution)/shard_map/ppermute | solution.py:19
  76.3 0.9 %copy-start.9 = (bf16[384,192]{0,1:T(8,128)(2,1)S(1)}, bf16[384,192]{0,1:T(8,128)(2,1)}, u32[]{:S(2)}) copy-start(bf16[384,192]{0,1:T(8,128)(2,1)} %param.41) | copy-start | bytes 442372
  76.3 1.0 %copy-start.13 = (bf16[192,192]{1,0:T(8,128)(2,1)S(1)}, bf16[192,192]{1,0:T(8,128)(2,1)}, u32[]{:S(2)}) copy-start(bf16[192,192]{1,0:T(8,128)(2,1)} %param.43) | copy-start | bytes 221188
  76.3 0.9 %copy-start.17 = (f32[192]{0:T(256)S(1)}, f32[192]{0:T(256)}, u32[]{:S(2)}) copy-start(f32[192]{0:T(256)} %param.42) | copy-start | bytes 2308
where the time goes:
time: 79.3 us; the launch traced here: 78.7 us
  starting transfers between devices  30.4 us (38%)
  waiting for transfers between devices  19.7 us (25%)
  matrix products  18.5 us (23%)
  other arithmetic  5.14 us (6%)
  local copies, waits for them, and re-layouts  3.47 us (4%)
  between operations  1.11 us (1%)
    ppermute x4, starting transfers between devices, padded_2(): lax.ppermute(lax.slice_in_dim(block, block.shape[dim] - width, None, axis...  15.8 us
    ppermute x4, waiting for transfers between devices, padded_2(): lax.ppermute(lax.slice_in_dim(block, 0, width, axis=dim), axis, backward)  10.6 us
    all_to_all x1, waiting for transfers between devices, body(): lax.all_to_all(buffer, 'py', split_axis=0, concat_axis=0, tiled=True)  8.83 us
    dot_general x12, matrix products, pick_rows(): jnp.dot(selector, table, preferred_element_type=jnp.float32)  7.2 us
    ppermute x4, starting transfers between devices, padded_2(): lax.ppermute(lax.slice_in_dim(block, 0, width, axis=dim), axis, backward)  6.43 us
    all_to_all x1, starting transfers between devices, body(): lax.all_to_all(member_ids, 'py', split_axis=0, concat_axis=0, tiled=True)  4.59 us
    all_to_all x1, starting transfers between devices, body(): lax.all_to_all(buffer, 'py', split_axis=0, concat_axis=0, tiled=True)  3.59 us
    dot_general x5, matrix products, add_block(): jnp.dot(hidden, weight_out, preferred_element_type=jnp.float32)  2.8 us
  transfers between devices with their start and end apart: 10, of which 5 were waited for; matrix products, arithmetic and copies ran while one was open for 27% of the time, Pallas kernels for 0%

commit v1 on v0

v1 whole, which is shorter than its diff:
```python
import functools
import math

import jax
import jax.numpy as jnp
from jax import lax
from jax.experimental import pallas as pl
from jax.experimental.pallas import tpu as pltpu
from jax.sharding import PartitionSpec as P

CLUST_DEV = 64
BF = jnp.bfloat16
F32 = jnp.float32
MESH = pl.DeviceIdType.MESH


def dot(a, b):
    return jnp.dot(a, b, preferred_element_type=F32)


def dot_nt(a, b):
    return lax.dot_general(a, b, (((1,), (1,)), ((), ())), preferred_element_type=F32)


def silu(x):
    half = 0.5 * x
    return half + half * jnp.tanh(half)


def normed(v, axis):
    scale = 1.0 / v.shape[axis]
    center = v - jnp.sum(v, axis=axis, keepdims=True) * scale
    var = jnp.sum(center * center, axis=axis, keepdims=True) * scale
    return center * lax.rsqrt(var + 1e-05)


def one_hot_columns(ids, first, count):
    rows = lax.broadcasted_iota(jnp.int32, (count, ids.shape[1]), 0)
    return jnp.where(rows == ids - first, 1.0, 0.0).astype(BF)


def column(ref):
    return jnp.broadcast_to(ref[...], (8, ref.shape[1])).T[:, :1]


def flip(ref):
    return ref[...].astype(F32).T.astype(BF)


def node_part(feats, incoming, in_ref, bias_ref, out_ref):
    joined = jnp.concatenate([feats, incoming], axis=0)
    hidden = silu(dot(in_ref[...], joined) + column(bias_ref)).astype(BF)
    return (feats.astype(F32) + normed(dot(flip(out_ref), hidden), 0)).astype(BF)


def kernel(
    n_px, n_py, chunk,
    feats_ref, src_ref, tgt_ref, send_ref, ew_ref, eb_ref, eo_ref, nw_ref, nb_ref, no_ref,
    owner_ref, member_ref, csend_ref, csrc_ref, ctgt_ref, cew_ref, ceb_ref, ceo_ref,
    cnw_ref, cnb_ref, cno_ref,
    out_ref, cout_ref,
    halo_out, halo_in, chalo_out, chalo_in, pool_out, pool_in, aug,
    at_own, bt, pre, ot, mt,
    h_send, h_recv, c_send, c_recv, p_send, p_recv,
):
    width, nd = feats_ref.shape
    edges = src_ref.shape[1]
    halo = send_ref.shape[1]
    cdev = cout_ref.shape[0]
    chalo = csend_ref.shape[1]
    mx, my = lax.axis_index("px"), lax.axis_index("py")

    barrier = pltpu.get_barrier_semaphore()
    for k in range(1, n_py):
        pl.semaphore_signal(
            barrier, inc=1, device_id=(mx, lax.rem(my + k, n_py)), device_id_type=MESH
        )

    @pl.when(mx > 0)
    def _():
        pl.semaphore_signal(barrier, inc=1, device_id=(mx - 1, my), device_id_type=MESH)

    @pl.when(mx < n_px - 1)
    def _():
        pl.semaphore_signal(barrier, inc=1, device_id=(mx + 1, my), device_id_type=MESH)

    arrives = (mx > 0, mx < n_px - 1, my > 0, my < n_py - 1)
    leaves = (mx < n_px - 1, mx > 0, my < n_py - 1, my > 0)
    goes_to = (
        (lax.rem(mx + 1, n_px), my),
        (lax.rem(mx + n_px - 1, n_px), my),
        (mx, lax.rem(my + 1, n_py)),
        (mx, lax.rem(my + n_py - 1, n_py)),
    )

    def halo_copy(slot, out, into, amount, send_sem, recv_sem):
        return pltpu.make_async_remote_copy(
            src_ref=out,
            dst_ref=into.at[pl.ds(slot * amount, amount)],
            send_sem=send_sem.at[slot],
            recv_sem=recv_sem.at[slot],
            device_id=goes_to[slot],
            device_id_type=MESH,
        )

    def halo_start(*where):
        for slot in range(4):
            @pl.when(leaves[slot])
            def _():
                halo_copy(slot, *where).start()

    def halo_zero(into, amount):
        for slot in range(4):
            @pl.when(jnp.logical_not(arrives[slot]))
            def _():
                into[slot * amount:(slot + 1) * amount, :] = jnp.zeros((amount, width), BF)

    def halo_arrived(*where):
        for slot in range(4):
            @pl.when(arrives[slot])
            def _():
                halo_copy(slot, *where).wait_recv()

    def halo_sent(*where):
        for slot in range(4):
            @pl.when(leaves[slot])
            def _():
                halo_copy(slot, *where).wait_send()

    feats = feats_ref[...]
    halo_out[...] = dot(feats, one_hot_columns(send_ref[...], 0, nd)).T.astype(BF)

    beside = jnp.where(mx > 0, 1, 0) + jnp.where(mx < n_px - 1, 1, 0)
    pl.semaphore_wait(barrier, n_py - 1 + beside)

    fine = (halo_out, halo_in, halo, h_send, h_recv)
    halo_start(*fine)
    halo_zero(halo_in, halo)
    halo_zero(chalo_in, chalo)

    at_own[...] = dot(ew_ref[:, :width], feats).astype(BF)
    bt[...] = (dot(ew_ref[:, width:], feats) + column(eb_ref)).astype(BF)
    aug[width:, :] = jnp.ones((aug.shape[0] - width, nd), BF)

    def first(step, carry):
        lanes = pl.ds(pl.multiple_of(step * chunk, chunk), chunk)
        target_hot = one_hot_columns(tgt_ref[:, lanes], 0, nd)
        ot[:, lanes] = target_hot
        source_hot = one_hot_columns(src_ref[:, lanes], 0, nd)
        pre[:, lanes] = dot(bt[...], target_hot) + dot(at_own[...], source_hot)
        return carry

    lax.fori_loop(0, edges // chunk, first, 0)

    halo_arrived(*fine)
    at_halo = dot_nt(ew_ref[:, :width], halo_in[...]).astype(BF)
    eo_t = flip(eo_ref)

    def second(step, carry):
        lanes = pl.ds(pl.multiple_of(step * chunk, chunk), chunk)
        source_hot = one_hot_columns(src_ref[:, lanes], nd, 4 * halo)
        hidden = silu(pre[:, lanes] + dot(at_halo, source_hot)).astype(BF)
        mt[:, lanes] = normed(dot(eo_t, hidden), 0).astype(BF)
        return carry

    lax.fori_loop(0, edges // chunk, second, 0)

    incoming = dot_nt(ot[...], mt[...]).T.astype(BF)
    updated = node_part(feats, incoming, nw_ref, nb_ref, no_ref)
    out_ref[...] = updated
    aug[:width, :] = updated

    cluster = owner_ref[...] * cdev + member_ref[...]
    partial = dot_nt(one_hot_columns(cluster, 0, n_py * cdev), aug[...]).astype(BF)
    for k in range(n_py):
        pool_out[k] = partial[k * cdev:(k + 1) * cdev]

    def pool_copy(k):
        peer = lax.rem(my + k, n_py)
        return pltpu.make_async_remote_copy(
            src_ref=pool_out.at[peer],
            dst_ref=pool_in.at[k - 1],
            send_sem=p_send.at[k - 1],
            recv_sem=p_recv.at[k - 1],
            device_id=(mx, peer),
            device_id_type=MESH,
        )

    for k in range(1, n_py):
        pool_copy(k).start()

    ct_hot = one_hot_columns(ctgt_ref[...], 0, cdev)
    cs_hot = one_hot_columns(csrc_ref[...], 0, cdev)
    ch_hot = one_hot_columns(csrc_ref[...], cdev, 4 * chalo)
    ceo_t = flip(ceo_ref)
    total = pool_out[my].astype(F32)
    halo_sent(*fine)

    for k in range(1, n_py):
        pool_copy(k).wait_recv()
        total = total + pool_in[k - 1].astype(F32)
    mean = total[:, :width] / jnp.maximum(total[:, width:width + 1], 1.0)
    coarse = mean.T.astype(BF)

    chalo_out[...] = dot(coarse, one_hot_columns(csend_ref[...], 0, cdev)).T.astype(BF)
    rough = (chalo_out, chalo_in, chalo, c_send, c_recv)
    halo_start(*rough)
    cat = dot(cew_ref[:, :width], coarse).astype(BF)
    cbt = (dot(cew_ref[:, width:], coarse) + column(ceb_ref)).astype(BF)
    cpre = dot(cbt, ct_hot) + dot(cat, cs_hot)
    for k in range(1, n_py):
        pool_copy(k).wait_send()
    halo_arrived(*rough)

    cah = dot_nt(cew_ref[:, :width], chalo_in[...]).astype(BF)
    chidden = silu(cpre + dot(cah, ch_hot)).astype(BF)
    cmt = normed(dot(ceo_t, chidden), 0).astype(BF)
    cincoming = dot_nt(ct_hot, cmt).T.astype(BF)
    cout_ref[...] = node_part(coarse, cincoming, cnw_ref, cnb_ref, cno_ref).astype(F32).T.astype(BF)
    halo_sent(*rough)


def body(n_px, n_py, *args):
    (node_features, edge_source, edge_target, halo_send, edge_weight_in, edge_bias,
     edge_weight_out, node_weight_in, node_bias, node_weight_out, cluster_owner, cluster_member,
     coarse_send, coarse_source, coarse_target, coarse_edge_in, coarse_edge_bias,
     coarse_edge_out, coarse_node_in, coarse_node_bias, coarse_node_out) = args
    nd, width = node_features.shape
    edges, halo, chalo = edge_source.shape[1], halo_send.shape[1], coarse_send.shape[1]
    wide = (width // 128 + 1) * 128
    chunk = math.gcd(edges, 512)
    row = lambda v: v.reshape(1, -1)
    ins = (
        node_features.T, edge_source, edge_target, halo_send, edge_weight_in.T, row(edge_bias),
        edge_weight_out, node_weight_in.T, row(node_bias), node_weight_out, row(cluster_owner),
        row(cluster_member), coarse_send, coarse_source, coarse_target, coarse_edge_in.T,
        row(coarse_edge_bias), coarse_edge_out, coarse_node_in.T, row(coarse_node_bias),
        coarse_node_out,
    )
    vmem = pl.BlockSpec(memory_space=pltpu.VMEM)
    fine, rough = pl.pallas_call(
        functools.partial(kernel, n_px, n_py, chunk),
        out_shape=(
            jax.ShapeDtypeStruct((width, nd), BF),
            jax.ShapeDtypeStruct((CLUST_DEV, width), BF),
        ),
        in_specs=[vmem] * len(ins),
        out_specs=(vmem, vmem),
        scratch_shapes=[
            pltpu.VMEM((halo, width), BF),
            pltpu.VMEM((4 * halo, width), BF),
            pltpu.VMEM((chalo, width), BF),
            pltpu.VMEM((4 * chalo, width), BF),
            pltpu.VMEM((n_py, CLUST_DEV, wide), BF),
            pltpu.VMEM((n_py - 1, CLUST_DEV, wide), BF),
            pltpu.VMEM((wide, nd), BF),
            pltpu.VMEM((width, nd), BF),
            pltpu.VMEM((width, nd), BF),
            pltpu.VMEM((width, edges), F32),
            pltpu.VMEM((nd, edges), BF),
            pltpu.VMEM((width, edges), BF),
            pltpu.SemaphoreType.DMA((4,)),
            pltpu.SemaphoreType.DMA((4,)),
            pltpu.SemaphoreType.DMA((4,)),
            pltpu.SemaphoreType.DMA((4,)),
            pltpu.SemaphoreType.DMA((n_py - 1,)),
            pltpu.SemaphoreType.DMA((n_py - 1,)),
        ],
        compiler_params=pltpu.CompilerParams(
            collective_id=0, has_side_effects=True, vmem_limit_bytes=40 * 1024 * 1024
        ),
    )(*ins)
    return fine.T, rough


def solution(mesh):
    split = P(("px", "py"), None)
    full = P()
    placed = (
        split, split, split, split, full, full, full, full, full, full,
        split, P(("px", "py")), split, split, split, full, full, full, full, full, full,
    )
    return jax.shard_map(
        functools.partial(body, mesh.shape["px"], mesh.shape["py"]),
        mesh=mesh,
        in_specs=placed,
        out_specs=(split, split),
        check_vma=False,
    )
```

time: 79.3 us -> 37.8 us (0.48)
  the two profiles are of different devices: /device:TPU:3 before, /device:TPU:0 now
where the time goes in v1:
time: 37.8 us; the launch traced here: 37.3 us
  Pallas kernels  23.1 us (61%)
  local copies, waits for them, and re-layouts  13.5 us (36%)
  between operations  0.72 us (2%)
    pallas_call x1, Pallas kernels, body(): pl.pallas_call(functools.partial(kernel, n_px, n_py, chunk), out_shape=(j...  23.1 us
    unnamed x44, local copies, waits for them, and re-layouts  13.5 us

profile of v1, /device:TPU:0, one launch (start us, length us, event | category | flops | bytes accessed | tf_op | source)
XLA Modules:
  0.0 37.3 jit_solution(13107719448557502069)
XLA Ops:
  0.6 0.0 copy-start.9
  0.6 0.0 copy-start.15
  0.7 0.0 copy-start.14
  0.7 0.0 copy-start.19
  0.7 0.0 copy-start.12
  0.7 0.0 copy-start.11
  0.7 0.0 copy-start.13
  0.7 0.6 %copy-done.9 = s32[1,3072]{1,0:T(1,128)S(1)} copy-done((s32[1,3072]{1,0:T(1,128)S(1)}, s32[1,3072]{1,0:T(1,128)}, u32[]{:S(2)}) %copy-start.9) | copy-done | bytes 12312
  1.3 0.0 copy-done.15
  1.4 0.0 copy-done.14
  1.4 0.0 copy-done.19
  1.4 0.0 copy-done.12
  1.4 0.0 copy-done.11
  1.4 0.0 copy-done.13
  1.4 0.0 copy-start
  1.4 0.9 %copy-done = bf16[512,192]{0,1:T(8,128)(2,1)S(1)} copy-done((bf16[512,192]{0,1:T(8,128)(2,1)S(1)}, bf16[512,192]{0,1:T(8,128)(2,1)}, u32[]{:S(2)}) %copy-start) | copy-done | bytes 196632
  2.3 0.0 copy-start.1
  2.3 0.9 %copy-done.1 = bf16[384,192]{0,1:T(8,128)(2,1)S(1)} copy-done((bf16[384,192]{0,1:T(8,128)(2,1)S(1)}, bf16[384,192]{0,1:T(8,128)(2,1)}, u32[]{:S(2)}) %copy-start.1) | copy-done | bytes 147480
  3.3 0.0 copy-start.2
  3.3 0.9 %copy-done.2 = bf16[384,192]{0,1:T(8,128)(2,1)S(1)} copy-done((bf16[384,192]{0,1:T(8,128)(2,1)S(1)}, bf16[384,192]{0,1:T(8,128)(2,1)}, u32[]{:S(2)}) %copy-start.2) | copy-done | bytes 147480
  4.2 0.0 copy-start.3
  4.2 0.9 %copy-done.3 = bf16[384,192]{0,1:T(8,128)(2,1)S(1)} copy-done((bf16[384,192]{0,1:T(8,128)(2,1)S(1)}, bf16[384,192]{0,1:T(8,128)(2,1)}, u32[]{:S(2)}) %copy-start.3) | copy-done | bytes 147480
  5.1 0.0 copy-start.4
  5.1 0.9 %copy-done.4 = bf16[384,192]{0,1:T(8,128)(2,1)S(1)} copy-done((bf16[384,192]{0,1:T(8,128)(2,1)S(1)}, bf16[384,192]{0,1:T(8,128)(2,1)}, u32[]{:S(2)}) %copy-start.4) | copy-done | bytes 147480
  6.0 0.0 copy-start.5
  6.0 0.9 %copy-done.5 = bf16[192,192]{1,0:T(8,128)(2,1)S(1)} copy-done((bf16[192,192]{1,0:T(8,128)(2,1)S(1)}, bf16[192,192]{1,0:T(8,128)(2,1)}, u32[]{:S(2)}) %copy-start.5) | copy-done | bytes 73752
  6.9 0.0 copy-start.6
  6.9 0.9 %copy-done.6 = bf16[192,192]{1,0:T(8,128)(2,1)S(1)} copy-done((bf16[192,192]{1,0:T(8,128)(2,1)S(1)}, bf16[192,192]{1,0:T(8,128)(2,1)}, u32[]{:S(2)}) %copy-start.6) | copy-done | bytes 73752
  7.8 0.0 copy-start.7
  7.8 0.9 %copy-done.7 = bf16[192,192]{1,0:T(8,128)(2,1)S(1)} copy-done((bf16[192,192]{1,0:T(8,128)(2,1)S(1)}, bf16[192,192]{1,0:T(8,128)(2,1)}, u32[]{:S(2)}) %copy-start.7) | copy-done | bytes 73752
  8.7 0.0 copy-start.8
  8.7 0.9 %copy-done.8 = bf16[192,192]{1,0:T(8,128)(2,1)S(1)} copy-done((bf16[192,192]{1,0:T(8,128)(2,1)S(1)}, bf16[192,192]{1,0:T(8,128)(2,1)}, u32[]{:S(2)}) %copy-start.8) | copy-done | bytes 73752
  9.6 0.0 copy-start.10
  9.6 0.7 %copy-done.10 = s32[1,3072]{1,0:T(1,128)S(1)} copy-done((s32[1,3072]{1,0:T(1,128)S(1)}, s32[1,3072]{1,0:T(1,128)}, u32[]{:S(2)}) %copy-start.10) | copy-done | bytes 12312
  10.3 0.0 copy-start.16
  10.3 0.7 %copy-done.16 = f32[192]{0:T(256)S(1)} copy-done((f32[192]{0:T(256)S(1)}, f32[192]{0:T(256)}, u32[]{:S(2)}) %copy-start.16) | copy-done | bytes 792
  10.9 0.0 copy-start.17
  10.9 0.7 %copy-done.17 = f32[192]{0:T(256)S(1)} copy-done((f32[192]{0:T(256)S(1)}, f32[192]{0:T(256)}, u32[]{:S(2)}) %copy-start.17) | copy-done | bytes 792
  11.6 0.0 copy-start.18
  11.6 0.7 %copy-done.18 = f32[192]{0:T(256)S(1)} copy-done((f32[192]{0:T(256)S(1)}, f32[192]{0:T(256)}, u32[]{:S(2)}) %copy-start.18) | copy-done | bytes 792
  12.3 0.0 copy-start.20
  12.3 0.7 %copy-done.20 = s32[1,16]{1,0:T(1,128)S(1)} copy-done((s32[1,16]{1,0:T(1,128)S(1)}, s32[1,16]{1,0:T(1,128)}, u32[]{:S(2)}) %copy-start.20) | copy-done | bytes 88
  13.0 23.1 %shard_map.212 = (bf16[192,512]{1,0:T(8,128)(2,1)S(1)}, bf16[64,192]{1,0:T(8,128)(2,1)S(1)}) custom-call(bf16[192,512]{1,0:T(8,128)(2,1)S(1)} %bitcast.12, s32[1,3072]{1,0:T(1,128)S(1)} %copy-done.9, s32[1,3072]{1,0:T(1,128)S(1)} %copy-done.10, s32[1,64]{1,0:T(1,128)S(1)} %copy-done.19, bf16[192,384]{1,0:T(8,128)(2,1)S(1)} %bitcast.14, ...), custom_call_target="tpu_custom_call" | custom-call | tf_op jit(solution)/shard_map/pallas_call | solution.py:241
  36.0 0.7 %copy.25 = bf16[512,192]{0,1:T(8,128)(2,1)} copy(bf16[512,192]{0,1:T(8,128)(2,1)S(1)} %bitcast.13) | data formatting | bytes 393216
  36.7 0.6 %copy.26 = bf16[64,192]{1,0:T(8,128)(2,1)} copy(bf16[64,192]{1,0:T(8,128)(2,1)S(1)} %get-tuple-element.9) | data formatting | bytes 49152
Async XLA Ops:
  0.6 0.7 %copy-start.9 = (s32[1,3072]{1,0:T(1,128)S(1)}, s32[1,3072]{1,0:T(1,128)}, u32[]{:S(2)}) copy-start(s32[1,3072]{1,0:T(1,128)} %src_ref.1) | copy-start | bytes 36868
  0.6 0.7 %copy-start.15 = (f32[192]{0:T(256)S(1)}, f32[192]{0:T(256)}, u32[]{:S(2)}) copy-start(f32[192]{0:T(256)} %param.26) | copy-start | bytes 2308
  0.7 0.7 %copy-start.14 = (s32[1,384]{1,0:T(1,128)S(1)}, s32[1,384]{1,0:T(1,128)}, u32[]{:S(2)}) copy-start(s32[1,384]{1,0:T(1,128)} %ctgt_ref.1) | copy-start | bytes 4612
  0.7 0.7 %copy-start.19 = (s32[1,64]{1,0:T(1,128)S(1)}, s32[1,64]{1,0:T(1,128)}, u32[]{:S(2)}) copy-start(s32[1,64]{1,0:T(1,128)} %send_ref.1) | copy-start | bytes 772
  0.7 0.7 %copy-start.12 = (s32[512]{0:T(512)S(1)}, s32[512]{0:T(512)}, u32[]{:S(2)}) copy-start(s32[512]{0:T(512)} %param.32) | copy-start | bytes 6148
  0.7 0.7 %copy-start.11 = (s32[512,1]{0,1:T(1,128)S(1)}, s32[512,1]{0,1:T(1,128)}, u32[]{:S(2)}) copy-start(s32[512,1]{0,1:T(1,128)} %param.31) | copy-start | bytes 6148
  0.7 0.7 %copy-start.13 = (s32[1,384]{1,0:T(1,128)S(1)}, s32[1,384]{1,0:T(1,128)}, u32[]{:S(2)}) copy-start(s32[1,384]{1,0:T(1,128)} %csrc_ref.1) | copy-start | bytes 4612
  1.4 0.9 %copy-start = (bf16[512,192]{0,1:T(8,128)(2,1)S(1)}, bf16[512,192]{0,1:T(8,128)(2,1)}, u32[]{:S(2)}) copy-start(bf16[512,192]{0,1:T(8,128)(2,1)} %param.21) | copy-start | bytes 589828
  2.3 0.9 %copy-start.1 = (bf16[384,192]{0,1:T(8,128)(2,1)S(1)}, bf16[384,192]{0,1:T(8,128)(2,1)}, u32[]{:S(2)}) copy-start(bf16[384,192]{0,1:T(8,128)(2,1)} %param.25) | copy-start | bytes 442372
  3.3 0.9 %copy-start.2 = (bf16[384,192]{0,1:T(8,128)(2,1)S(1)}, bf16[384,192]{0,1:T(8,128)(2,1)}, u32[]{:S(2)}) copy-start(bf16[384,192]{0,1:T(8,128)(2,1)} %param.28) | copy-start | bytes 442372
  4.2 0.9 %copy-start.3 = (bf16[384,192]{0,1:T(8,128)(2,1)S(1)}, bf16[384,192]{0,1:T(8,128)(2,1)}, u32[]{:S(2)}) copy-start(bf16[384,192]{0,1:T(8,128)(2,1)} %param.36) | copy-start | bytes 442372
  5.1 0.9 %copy-start.4 = (bf16[384,192]{0,1:T(8,128)(2,1)S(1)}, bf16[384,192]{0,1:T(8,128)(2,1)}, u32[]{:S(2)}) copy-start(bf16[384,192]{0,1:T(8,128)(2,1)} %param.39) | copy-start | bytes 442372
  6.0 0.9 %copy-start.5 = (bf16[192,192]{1,0:T(8,128)(2,1)S(1)}, bf16[192,192]{1,0:T(8,128)(2,1)}, u32[]{:S(2)}) copy-start(bf16[192,192]{1,0:T(8,128)(2,1)} %eo_ref.1) | copy-start | bytes 221188
  6.9 0.9 %copy-start.6 = (bf16[192,192]{1,0:T(8,128)(2,1)S(1)}, bf16[192,192]{1,0:T(8,128)(2,1)}, u32[]{:S(2)}) copy-start(bf16[192,192]{1,0:T(8,128)(2,1)} %no_ref.1) | copy-start | bytes 221188
  7.8 0.9 %copy-start.7 = (bf16[192,192]{1,0:T(8,128)(2,1)S(1)}, bf16[192,192]{1,0:T(8,128)(2,1)}, u32[]{:S(2)}) copy-start(bf16[192,192]{1,0:T(8,128)(2,1)} %ceo_ref.1) | copy-start | bytes 221188
  8.7 0.9 %copy-start.8 = (bf16[192,192]{1,0:T(8,128)(2,1)S(1)}, bf16[192,192]{1,0:T(8,128)(2,1)}, u32[]{:S(2)}) copy-start(bf16[192,192]{1,0:T(8,128)(2,1)} %cno_ref.1) | copy-start | bytes 221188
  9.6 0.7 %copy-start.10 = (s32[1,3072]{1,0:T(1,128)S(1)}, s32[1,3072]{1,0:T(1,128)}, u32[]{:S(2)}) copy-start(s32[1,3072]{1,0:T(1,128)} %tgt_ref.1) | copy-start | bytes 36868
  10.3 0.7 %copy-start.16 = (f32[192]{0:T(256)S(1)}, f32[192]{0:T(256)}, u32[]{:S(2)}) copy-start(f32[192]{0:T(256)} %param.29) | copy-start | bytes 2308
  10.9 0.7 %copy-start.17 = (f32[192]{0:T(256)S(1)}, f32[192]{0:T(256)}, u32[]{:S(2)}) copy-start(f32[192]{0:T(256)} %param.37) | copy-start | bytes 2308
  11.6 0.7 %copy-start.18 = (f32[192]{0:T(256)S(1)}, f32[192]{0:T(256)}, u32[]{:S(2)}) copy-start(f32[192]{0:T(256)} %param.40) | copy-start | bytes 2308
  12.3 0.7 %copy-start.20 = (s32[1,16]{1,0:T(1,128)S(1)}, s32[1,16]{1,0:T(1,128)}, u32[]{:S(2)}) copy-start(s32[1,16]{1,0:T(1,128)} %csend_ref.1) | copy-start | bytes 196

commit v2 on v1

--- a/solution.py
+++ b/solution.py
@@ -53,16 +53,30 @@
     return (feats.astype(F32) + normed(dot(flip(out_ref), hidden), 0)).astype(BF)
 
 
-def kernel(
-    n_px, n_py, chunk,
-    feats_ref, src_ref, tgt_ref, send_ref, ew_ref, eb_ref, eo_ref, nw_ref, nb_ref, no_ref,
-    owner_ref, member_ref, csend_ref, csrc_ref, ctgt_ref, cew_ref, ceb_ref, ceo_ref,
-    cnw_ref, cnb_ref, cno_ref,
-    out_ref, cout_ref,
-    halo_out, halo_in, chalo_out, chalo_in, pool_out, pool_in, aug,
-    at_own, bt, pre, ot, mt,
-    h_send, h_recv, c_send, c_recv, p_send, p_recv,
-):
+def kernel(n_px, n_py, chunk, *refs):
+    (
+        given, outs, (out_ref, cout_ref), held,
+        (halo_out, halo_in, chalo_out, chalo_in, pool_out, pool_in, aug),
+        (at_own, bt, pre, ot),
+        (in_sem, out_sem, h_send, h_recv, c_send, c_recv, p_send, p_recv),
+    ) = (refs[:21], refs[21:23], refs[23:25], refs[25:46], refs[46:53], refs[53:57], refs[57:])
+    (
+        feats_ref, src_ref, tgt_ref, send_ref, ew_ref, eb_ref, eo_ref, nw_ref, nb_ref, no_ref,
+        owner_ref, member_ref, csend_ref, csrc_ref, ctgt_ref, cew_ref, ceb_ref, ceo_ref,
+        cnw_ref, cnb_ref, cno_ref,
+    ) = held
+
+    def load(k):
+        return pltpu.make_async_copy(given[k], held[k], in_sem.at[k])
+
+    def loaded(*which):
+        for k in which:
+            load(k).wait()
+
+    early = (0, 3, 4, 5, 2, 1)
+    for k in early:
+        load(k).start()
+
     width, nd = feats_ref.shape
     edges = src_ref.shape[1]
     halo = send_ref.shape[1]
@@ -83,6 +97,10 @@
     @pl.when(mx < n_px - 1)
     def _():
         pl.semaphore_signal(barrier, inc=1, device_id=(mx + 1, my), device_id_type=MESH)
+
+    for k in range(21):
+        if k not in early:
+            load(k).start()
 
     arrives = (mx > 0, mx < n_px - 1, my > 0, my < n_py - 1)
     leaves = (mx < n_px - 1, mx > 0, my < n_py - 1, my > 0)
@@ -127,6 +145,7 @@
             def _():
                 halo_copy(slot, *where).wait_send()
 
+    loaded(0, 3)
     feats = feats_ref[...]
     halo_out[...] = dot(feats, one_hot_columns(send_ref[...], 0, nd)).T.astype(BF)
 
@@ -138,37 +157,39 @@
     halo_zero(halo_in, halo)
     halo_zero(chalo_in, chalo)
 
+    loaded(4, 5)
     at_own[...] = dot(ew_ref[:, :width], feats).astype(BF)
     bt[...] = (dot(ew_ref[:, width:], feats) + column(eb_ref)).astype(BF)
     aug[width:, :] = jnp.ones((aug.shape[0] - width, nd), BF)
 
-    def first(step, carry):
-        lanes = pl.ds(pl.multiple_of(step * chunk, chunk), chunk)
-        target_hot = one_hot_columns(tgt_ref[:, lanes], 0, nd)
-        ot[:, lanes] = target_hot
-        source_hot = one_hot_columns(src_ref[:, lanes], 0, nd)
-        pre[:, lanes] = dot(bt[...], target_hot) + dot(at_own[...], source_hot)
-        return carry
-
-    lax.fori_loop(0, edges // chunk, first, 0)
-
+    loaded(2, 1)
+    for at in range(0, edges, chunk):
+        target_hot = one_hot_columns(tgt_ref[:, at:at + chunk], 0, nd)
+        ot[:, at:at + chunk] = target_hot
+        source_hot = one_hot_columns(src_ref[:, at:at + chunk], 0, nd)
+        pre[:, at:at + chunk] = dot(bt[...], target_hot) + dot(at_own[...], source_hot)
+
+    loaded(*range(6, 21))
+    eo_t = flip(eo_ref)
     halo_arrived(*fine)
     at_halo = dot_nt(ew_ref[:, :width], halo_in[...]).astype(BF)
-    eo_t = flip(eo_ref)
-
-    def second(step, carry):
-        lanes = pl.ds(pl.multiple_of(step * chunk, chunk), chunk)
-        source_hot = one_hot_columns(src_ref[:, lanes], nd, 4 * halo)
-        hidden = silu(pre[:, lanes] + dot(at_halo, source_hot)).astype(BF)
-        mt[:, lanes] = normed(dot(eo_t, hidden), 0).astype(BF)
-        return carry
-
-    lax.fori_loop(0, edges // chunk, second, 0)
-
-    incoming = dot_nt(ot[...], mt[...]).T.astype(BF)
+
+    totals = jnp.zeros((nd, width), F32)
+    for at in range(0, edges, chunk):
+        source_hot = one_hot_columns(src_ref[:, at:at + chunk], nd, 4 * halo)
+        hidden = silu(pre[:, at:at + chunk] + dot(at_halo, source_hot)).astype(BF)
+        message = normed(dot(eo_t, hidden), 0).astype(BF)
+        totals = totals + dot_nt(ot[:, at:at + chunk], message)
+
+    incoming = totals.T.astype(BF)
     updated = node_part(feats, incoming, nw_ref, nb_ref, no_ref)
     out_ref[...] = updated
     aug[:width, :] = updated
+    stores = [
+        pltpu.make_async_copy(made, to, out_sem.at[k])
+        for k, (made, to) in enumerate(zip((out_ref, cout_ref), outs))
+    ]
+    stores[0].start()
 
     cluster = owner_ref[...] * cdev + member_ref[...]
     partial = dot_nt(one_hot_columns(cluster, 0, n_py * cdev), aug[...]).astype(BF)
@@ -217,7 +238,10 @@
     cmt = normed(dot(ceo_t, chidden), 0).astype(BF)
     cincoming = dot_nt(ct_hot, cmt).T.astype(BF)
     cout_ref[...] = node_part(coarse, cincoming, cnw_ref, cnb_ref, cno_ref).astype(F32).T.astype(BF)
+    stores[1].start()
     halo_sent(*rough)
+    for store in stores:
+        store.wait()
 
 
 def body(n_px, n_py, *args):
@@ -237,16 +261,17 @@
         row(coarse_edge_bias), coarse_edge_out, coarse_node_in.T, row(coarse_node_bias),
         coarse_node_out,
     )
-    vmem = pl.BlockSpec(memory_space=pltpu.VMEM)
+    hbm = pl.BlockSpec(memory_space=pltpu.HBM)
     fine, rough = pl.pallas_call(
         functools.partial(kernel, n_px, n_py, chunk),
         out_shape=(
             jax.ShapeDtypeStruct((width, nd), BF),
             jax.ShapeDtypeStruct((CLUST_DEV, width), BF),
         ),
-        in_specs=[vmem] * len(ins),
-        out_specs=(vmem, vmem),
-        scratch_shapes=[
+        in_specs=[hbm] * len(ins),
+        out_specs=(hbm, hbm),
+        scratch_shapes=[pltpu.VMEM((width, nd), BF), pltpu.VMEM((CLUST_DEV, width), BF)]
+        + [pltpu.VMEM(v.shape, v.dtype) for v in ins] + [
             pltpu.VMEM((halo, width), BF),
             pltpu.VMEM((4 * halo, width), BF),
             pltpu.VMEM((chalo, width), BF),
@@ -258,7 +283,8 @@
             pltpu.VMEM((width, nd), BF),
             pltpu.VMEM((width, edges), F32),
             pltpu.VMEM((nd, edges), BF),
-            pltpu.VMEM((width, edges), BF),
+            pltpu.SemaphoreType.DMA((len(ins),)),
+            pltpu.SemaphoreType.DMA((2,)),
             pltpu.SemaphoreType.DMA((4,)),
             pltpu.SemaphoreType.DMA((4,)),
             pltpu.SemaphoreType.DMA((4,)),
@@ -267,7 +293,7 @@
             pltpu.SemaphoreType.DMA((n_py - 1,)),
         ],
         compiler_params=pltpu.CompilerParams(
-            collective_id=0, has_side_effects=True, vmem_limit_bytes=40 * 1024 * 1024
+            collective_id=0, has_side_effects=True, vmem_limit_bytes=64 * 1024 * 1024
         ),
     )(*ins)
     return fine.T, rough

time: 37.8 us -> 26.1 us (0.69)
  local copies, waits for them, and re-layouts: 13.5 us -> 2.24 us
    unnamed x44 -> x4, local copies, waits for them, and re-layouts: 13.5 us -> 2.24 us
where the time goes in v2:
time: 26.1 us; the launch traced here: 25.9 us
  Pallas kernels  23 us (88%)
  local copies, waits for them, and re-layouts  2.24 us (9%)
  between operations  0.66 us (3%)
    pallas_call x1, Pallas kernels, body(): pl.pallas_call(functools.partial(kernel, n_px, n_py, chunk), out_shape=(j...  23 us
    unnamed x4, local copies, waits for them, and re-layouts  2.24 us

profile of v2, /device:TPU:0, one launch (start us, length us, event | category | flops | bytes accessed | tf_op | source)
XLA Modules:
  0.0 25.9 jit_solution(5048339427210373823)
XLA Ops:
  0.6 23.0 %shard_map.212 = (bf16[192,512]{1,0:T(8,128)(2,1)}, bf16[64,192]{1,0:T(8,128)(2,1)}) custom-call(bf16[192,512]{1,0:T(8,128)(2,1)} %bitcast.12, s32[1,3072]{1,0:T(1,128)} %refs_1_.1, s32[1,3072]{1,0:T(1,128)} %refs_2_.1, s32[1,64]{1,0:T(1,128)} %refs_3_.1, bf16[192,384]{1,0:T(8,128)(2,1)} %bitcast.14, f32[1,192]{1,0:T(1,128)} %bitcast.20, ...), custom_call_target="tpu_custom_call" | custom-call | tf_op jit(solution)/shard_map/pallas_call | solution.py:265
  23.6 0.0 copy-start
  23.7 1.6 %copy.25 = bf16[512,192]{0,1:T(8,128)(2,1)} copy(bf16[512,192]{0,1:T(8,128)(2,1)} %bitcast.13) | data formatting | bytes 393216
  25.3 0.0 copy-done
  25.3 0.6 %copy.26 = bf16[64,192]{1,0:T(8,128)(2,1)} copy(bf16[64,192]{1,0:T(8,128)(2,1)S(1)} %copy-done) | data formatting | bytes 49152
Async XLA Ops:
  23.6 1.6 %copy-start = (bf16[64,192]{1,0:T(8,128)(2,1)S(1)}, bf16[64,192]{1,0:T(8,128)(2,1)}, u32[]{:S(2)}) copy-start(bf16[64,192]{1,0:T(8,128)(2,1)} %get-tuple-element.9) | copy-start | bytes 73732

commit v3 on v2

--- a/solution.py
+++ b/solution.py
@@ -35,8 +35,10 @@
 
 
 def one_hot_columns(ids, first, count):
-    rows = lax.broadcasted_iota(jnp.int32, (count, ids.shape[1]), 0)
-    return jnp.where(rows == ids - first, 1.0, 0.0).astype(BF)
+    shape = (count, ids.shape[1])
+    rows = lax.broadcasted_iota(jnp.int16, shape, 0)
+    wanted = jnp.broadcast_to((ids - first).astype(jnp.int16), shape)
+    return jnp.where(rows == wanted, jnp.ones(shape, BF), jnp.zeros(shape, BF))
 
 
 def column(ref):
@@ -265,11 +267,11 @@
     fine, rough = pl.pallas_call(
         functools.partial(kernel, n_px, n_py, chunk),
         out_shape=(
-            jax.ShapeDtypeStruct((width, nd), BF),
-            jax.ShapeDtypeStruct((CLUST_DEV, width), BF),
+            pltpu.VMEM((width, nd), BF),
+            pltpu.VMEM((CLUST_DEV, width), BF),
         ),
         in_specs=[hbm] * len(ins),
-        out_specs=(hbm, hbm),
+        out_specs=(pl.BlockSpec(memory_space=pltpu.VMEM),) * 2,
         scratch_shapes=[pltpu.VMEM((width, nd), BF), pltpu.VMEM((CLUST_DEV, width), BF)]
         + [pltpu.VMEM(v.shape, v.dtype) for v in ins] + [
             pltpu.VMEM((halo, width), BF),
@@ -293,7 +295,7 @@
             pltpu.SemaphoreType.DMA((n_py - 1,)),
         ],
         compiler_params=pltpu.CompilerParams(
-            collective_id=0, has_side_effects=True, vmem_limit_bytes=64 * 1024 * 1024
+            collective_id=0, has_side_effects=True, vmem_limit_bytes=64 * 1024 * 1024 - 512 * 1024
         ),
     )(*ins)
     return fine.T, rough

time: 26.1 us -> 24.9 us (0.954)
  local copies, waits for them, and re-layouts: 2.24 us -> 1.29 us
    unnamed x4 -> x2, local copies, waits for them, and re-layouts: 2.24 us -> 1.29 us
where the time goes in v3:
time: 24.9 us; the launch traced here: 24.7 us
  Pallas kernels  22.8 us (92%)
  local copies, waits for them, and re-layouts  1.29 us (5%)
  between operations  0.65 us (3%)
    pallas_call x1, Pallas kernels, body(): pl.pallas_call(functools.partial(kernel, n_px, n_py, chunk), out_shape=(p...  22.8 us
    unnamed x2, local copies, waits for them, and re-layouts  1.29 us

profile of v3, /device:TPU:0, one launch (start us, length us, event | category | flops | bytes accessed | tf_op | source)
XLA Modules:
  0.0 24.7 jit_solution(8211141011547402204)
XLA Ops:
  0.6 22.8 %shard_map.212 = (bf16[192,512]{1,0:T(8,128)(2,1)S(1)}, bf16[64,192]{1,0:T(8,128)(2,1)S(1)}) custom-call(bf16[192,512]{1,0:T(8,128)(2,1)} %bitcast.13, s32[1,3072]{1,0:T(1,128)} %refs_1_.1, s32[1,3072]{1,0:T(1,128)} %refs_2_.1, s32[1,64]{1,0:T(1,128)} %refs_3_.1, bf16[192,384]{1,0:T(8,128)(2,1)} %bitcast.14, f32[1,192]{1,0:T(1,128)} %bitcast.20, ...), custom_call_target="tpu_custom_call" | custom-call | tf_op jit(solution)/shard_map/pallas_call | solution.py:267
  23.4 0.7 %copy.25 = bf16[512,192]{0,1:T(8,128)(2,1)} copy(bf16[512,192]{0,1:T(8,128)(2,1)S(1)} %bitcast.12) | data formatting | bytes 393216
  24.1 0.6 %copy.26 = bf16[64,192]{1,0:T(8,128)(2,1)} copy(bf16[64,192]{1,0:T(8,128)(2,1)S(1)} %get-tuple-element.7) | data formatting | bytes 49152
